TPU v7x, 256 devices: a whole 4x4x8 slice. The times are simulated.
256 devices in a mesh: row: 32 (over x_hi, z, core), col: 8 (over y, x_lo).
Axes of the slice: x: 4 (x_hi: 2, x_lo: 2; x = x_hi * 2 + x_lo), y: 4, z: 8, core: 2. Of those that a mesh axis runs over, the one named last changes fastest.
Arguments:
- features: bfloat16 [65536, 128], P(('col', 'row')), may hold values from -6 to 6
- weight: bfloat16 [128, 256], replicated, may hold values from -0.5 to 0.5
- bias: float32 [256], replicated, may hold values from -3 to 3
- tile_values: bfloat16 [32, 8, 128, 128, 128], P('row', 'col'), may hold values from -0.1875 to 0.1875
- tile_row: int32 [32, 8, 128], P('row', 'col'), may hold values from 0 to 15
- tile_col: int32 [32, 8, 128], P('row', 'col'), may hold values from 0 to 63
- tile_count: int32 [32, 8], P('row', 'col'), may hold values from 1 to 128, as said below
- cotangent: bfloat16 [65536, 256], P(('row', 'col')), may hold values from -6 to 6
Outputs:
- output: bfloat16 [65536, 256], P(('row', 'col'))
- grad_features: bfloat16 [65536, 128], P(('col', 'row'))
- grad_weight: float32 [128, 256], replicated
- grad_bias: float32 [256], replicated
Inputs may be any that keep to these rules, and one draw needn't show every extreme that they name: Slots from tile_count on are ignored; some device has 128 live slots and some has 1. A device may list a tile more than once; the entries then add.
All inputs are finite; a program needn't handle non-finite values.
Results may differ from a plain program's by a relative error of at most 0.02.
Values may be sent and summed in bfloat16 or wider, within the bound.
A program may use at most 64 MiB of HBM per device.

v0:
```python
import math

import jax
import jax.numpy as jnp
from jax import lax
from jax.sharding import PartitionSpec as P


def slope(pre):
    sig = jax.nn.sigmoid(pre)
    return sig * (1.0 + pre * (1.0 - sig))


def split_product(data, matrix):
    upper = data.astype(jnp.bfloat16)
    lower = (data - upper.astype(jnp.float32)).astype(jnp.bfloat16)
    result = jnp.dot(upper, matrix, preferred_element_type=jnp.float32)
    return result + jnp.dot(lower, matrix, preferred_element_type=jnp.float32)


def tile_products(tiles, slot_rows, slot_cols, count, source, out_blocks, transposed):
    side = tiles.shape[-1]
    block_size = math.gcd(tiles.shape[0], 32)
    width = source.shape[-1]
    source_blocks = source.reshape(-1, side, width)
    turns = (count + block_size - 1) // block_size

    def step(turn, total):
        start = turn * block_size
        values_here = lax.dynamic_slice_in_dim(tiles, start, block_size, 0)
        rows_here = lax.dynamic_slice_in_dim(slot_rows, start, block_size, 0)
        cols_here = lax.dynamic_slice_in_dim(slot_cols, start, block_size, 0)
        live = start + jnp.arange(block_size, dtype=jnp.int32) < count
        if transposed:
            pieces = source_blocks[rows_here]
            contrib = jnp.einsum(
                "kij,kih->kjh", values_here, pieces, preferred_element_type=jnp.float32
            )
            target = cols_here
        else:
            pieces = source_blocks[cols_here]
            upper = pieces.astype(jnp.bfloat16)
            lower = (pieces - upper.astype(jnp.float32)).astype(jnp.bfloat16)
            contrib = jnp.einsum(
                "kij,kjh->kih", values_here, upper, preferred_element_type=jnp.float32
            )
            contrib = contrib + jnp.einsum(
                "kij,kjh->kih", values_here, lower, preferred_element_type=jnp.float32
            )
            target = rows_here
        contrib = jnp.where(live[:, None, None], contrib, jnp.zeros_like(contrib))
        return total.at[target].add(contrib)

    result = lax.fori_loop(0, turns, step, jnp.zeros((out_blocks, side, width), jnp.float32))
    return result.reshape(out_blocks * side, width)


def reduce_rows(partial_value, rows_here):
    whole = lax.psum(partial_value.astype(jnp.bfloat16), "col").astype(jnp.float32)
    return lax.dynamic_slice_in_dim(whole, lax.axis_index("col") * rows_here, rows_here, 0)


def local(features, weight, bias, tile_values, tile_row, tile_col, tile_count, cotangent):
    rows_here = features.shape[0]
    n_row = lax.axis_size("row")
    n_col = lax.axis_size("col")
    tiles = tile_values.reshape(tile_values.shape[2:])
    side = tiles.shape[-1]
    slot_rows = tile_row.reshape(-1)
    slot_cols = tile_col.reshape(-1)
    count = tile_count.reshape(())
    row_blocks = n_col * rows_here // side
    col_blocks = n_row * rows_here // side
    weight_back = weight.T
    values = jnp.dot(features, weight, preferred_element_type=jnp.float32)
    panel = lax.all_gather(values.astype(jnp.bfloat16), "row", axis=0, tiled=True).astype(
        values.dtype
    )
    partial_value = tile_products(tiles, slot_rows, slot_cols, count, panel, row_blocks, False)
    summed = reduce_rows(partial_value, rows_here)
    pre = summed + bias
    output = jax.nn.silu(pre).astype(jnp.bfloat16)
    grad_pre = (cotangent.astype(jnp.float32) * slope(pre)).astype(jnp.bfloat16)
    grad_rows = lax.all_gather(grad_pre, "col", axis=0, tiled=True)
    backward = tile_products(tiles, slot_rows, slot_cols, count, grad_rows, col_blocks, True)
    factor = (n_row * n_col * rows_here) ** (-0.5)
    grad_values = lax.psum_scatter(
        backward.astype(jnp.bfloat16), "row", scatter_dimension=0, tiled=True
    ).astype(jnp.float32)
    grad_features = split_product(grad_values, weight_back)
    local_weight = jnp.dot(
        features.astype(jnp.float32).T, grad_values, precision=lax.Precision.HIGHEST
    )
    local_bias = jnp.sum(grad_pre.astype(jnp.float32), axis=0)
    grad_weight, grad_bias = lax.psum((local_weight, local_bias), ("row", "col"))
    return (output, grad_features.astype(jnp.bfloat16), grad_weight * factor, grad_bias * factor)


def solution(mesh):
    placed = (
        P(("col", "row"), None),
        P(),
        P(),
        P("row", "col", None, None, None),
        P("row", "col", None),
        P("row", "col", None),
        P("row", "col"),
        P(("row", "col"), None),
    )
    return jax.shard_map(
        local,
        mesh=mesh,
        in_specs=placed,
        out_specs=(P(("row", "col"), None), P(("col", "row"), None), P(), P()),
        check_vma=False,
    )
```

profile of v0, /device:TPU:1, one launch (start us, length us, event | category | flops | bytes accessed | tf_op | source)
XLA Modules:
  0.0 765.3 jit_solution(7324063921551716936)
XLA Ops:
  7.2 0.0 copy-start
  7.2 0.0 all-gather.3.cloned.1.call-start
  7.2 0.8 copy-done
  8.0 1.7 convolution_convert_fusion
  9.7 0.0 all-gather.3.cloned.1.call-update
  9.7 0.0 all-reduce.3.cloned.1.call-start
  10.4 92.0 %all-gather.3.cloned.1.call-done = bf16[8192,256]{1,0:T(8,128)(2,1)} async-done(((bf16[256,256]{1,0:T(8,128)(2,1)}), bf16[8192,256]{1,0:T(8,128)(2,1)}) %all-gather.3.cloned.1.call-update) | async-done | bytes 4194320 | tf_op jit(solution)/shard_map/all_gather | solution.py:76
  102.4 6.6 convert.1
  109.0 0.2 broadcast_in_dim.34
  109.3 21.1 %while.20 = (s32[]{:T(128)}, f32[16,128,256]{2,1,0:T(8,128)S(1)}, s32[]{:T(128)}, s32[128]{0:T(128)S(1)}, s32[]{:T(128)}, /*index=5*/bf16[128,128,128]{2,1,0:T(8...) while((s32[]{:T(128)}, f32[16,128,256]{2,1,0:T(8,128)S(1)}, ...), condition=%wide.region_2.3_spmd, body=%wide.region_0.2_spmd.sunk | while | flops 545260800 | bytes 60822676 | solution.py:54
  109.3 0.7 add_compare_fusion.4
  109.9 0.1 compare_select_fusion.6
  110.0 6.2 gather_fusion
  116.2 3.3 fusion.28
  119.5 0.4 copy-done.1
  119.9 3.9 add_select_fusion.2
  123.8 6.5 scatter_fusion
  130.3 0.0 copy-start.4
  130.3 0.0 copy-start.7
  130.3 1.2 convert_element_type.53
  131.5 0.0 all-reduce.3.cloned.1.call-update
  131.5 0.0 all-gather.5.cloned.1.call-start
  131.6 140.4 %all-reduce.3.cloned.1.call-done = bf16[2048,256]{1,0:T(8,128)(2,1)} async-done(((bf16[2048,256]{1,0:T(8,128)(2,1)}), bf16[2048,256]{1,0:T(8,128)(2,1)}) %all-reduce.3.cloned.1.call-update) | async-done | bytes 1048592 | tf_op jit(solution)/shard_map/psum | solution.py:59
  272.0 1.7 convert_reduce_fusion
  273.7 0.0 all-gather.5.cloned.1.call-update
  273.7 0.0 reduce-scatter.2.cloned.1.call-start
  273.8 6.4 copy.12
  280.2 35.9 %all-gather.5.cloned.1.call-done = bf16[2048,256]{1,0:T(8,128)(2,1)} async-done(((bf16[256,256]{1,0:T(8,128)(2,1)}), bf16[2048,256]{1,0:T(8,128)(2,1)}) %all-gather.5.cloned.1.call-update) | async-done | bytes 1048592 | tf_op jit(solution)/shard_map/all_gather | solution.py:84
  316.1 4.3 broadcast_in_dim.35
  320.3 15.4 %while.21 = (s32[]{:T(128)}, f32[64,128,256]{2,1,0:T(8,128)}, s32[]{:T(128)}, s32[128]{0:T(128)S(1)}, s32[]{:T(128)}, /*index=5*/bf16[128,128,128]{1,2,0:T(8,128...) while((s32[]{:T(128)}, f32[64,128,256]{2,1,0:T(8,128)}, ...), condition=%wide.region_6.7_spmd, body=%wide.region_4.6_spmd.sunk | while | flops 270533888 | bytes 24122484 | solution.py:54
  320.3 0.7 add_compare_fusion.5
  321.0 0.1 compare_select_fusion.7
  321.1 0.7 gather_fusion.1
  321.8 3.9 convolution_select_fusion.2
  325.6 10.1 %scatter_fusion.1 = f32[64,128,256]{2,1,0:T(8,128)} fusion(f32[64,128,256]{2,1,0:T(8,128)} %get-tuple-element.300, s32[32]{0:T(128)S(1)} %get-tuple-element.249, f32[32,128,256]{2,1,0:T(8,128)} %convolution_select_fusion.2), kind=kCustom, calls=%fused_computation.3.clone.1 | custom fusion | flops 1048576 | bytes 12583040 | tf_op jit(solution)/shard_map/while/body/scatter-add | solution.py:52
  335.7 6.0 convert_element_type.59
  341.7 0.0 reduce-scatter.2.cloned.1.call-update
  341.7 0.0 all-reduce.5.cloned.1.call-start
  341.7 119.3 %psum.23 = f32[256]{0:T(256)S(1)} all-reduce(f32[256]{0:T(256)S(1)} %get-tuple-element.136), channel_id=1, replica_groups=mesh['row'=32,'col'=8] {'row','col'}, use_global_device_ids=true, to_apply=%region_10.11 | all-reduce | flops 256 | bytes 2048 | tf_op jit(solution)/shard_map/psum | solution.py:95
  461.0 0.6 broadcast_multiply_fusion.1
  461.6 45.0 %reduce-scatter.2.cloned.1.call-done = bf16[256,256]{1,0:T(8,128)(2,1)} async-done(((bf16[8192,256]{1,0:T(8,128)(2,1)}), bf16[256,256]{1,0:T(8,128)(2,1)}) %reduce-scatter.2.cloned.1.call-update) | async-done | bytes 131088 | tf_op jit(solution)/shard_map/reduce_scatter | solution.py:87
  506.6 1.8 convolution_bitcast_fusion
  508.4 0.0 all-reduce.5.cloned.1.call-update
  508.4 1.1 fusion.10
  509.5 1.7 fusion.9
  511.2 245.9 %all-reduce.5.cloned.1.call-done = f32[128,256]{0,1:T(8,128)} async-done(((f32[128,256]{0,1:T(8,128)}), f32[128,256]{0,1:T(8,128)}) %all-reduce.5.cloned.1.call-update) | async-done | bytes 131088 | tf_op jit(solution)/shard_map/psum | solution.py:95
  757.1 0.9 broadcast_multiply_fusion
  758.0 0.8 copy.14
  (13 shorter events, 0.0 us)
Async XLA Ops:
  7.2 0.8 copy-start
  7.2 95.3 %all-gather.3.cloned.1.call-start = ((), (), s32[]{:S(2)}) async-start(), calls=%async_computation.1 | async-start | bytes 4325376 | tf_op jit(solution)/shard_map/all_gather | solution.py:76
  9.7 262.3 %all-reduce.3.cloned.1.call-start = ((), (), s32[]{:S(2)}) async-start(), calls=%async_computation.2 | async-start | bytes 2097152 | tf_op jit(solution)/shard_map/psum | solution.py:59
  102.4 6.8 copy-start.5
  102.4 6.8 copy-start.6
  116.2 3.7 copy-start.1
  130.3 141.7 %copy-start.4 = (bf16[256,256]{1,0:T(8,128)(2,1)S(1)}, bf16[256,256]{1,0:T(8,128)(2,1)}, u32[]{:S(2)}) copy-start(bf16[256,256]{1,0:T(8,128)(2,1)} %param.19) | copy-start | bytes 393220
  130.3 141.6 %copy-start.7 = (f32[256]{0:T(256)S(1)}, f32[256]{0:T(256)}, u32[]{:S(2)}) copy-start(f32[256]{0:T(256)} %param.14) | copy-start | bytes 3076
  131.5 184.5 %all-gather.5.cloned.1.call-start = ((), (), s32[]{:S(2)}) async-start(), calls=%async_computation.3 | async-start | bytes 1179648 | tf_op jit(solution)/shard_map/all_gather | solution.py:84
  273.7 232.9 %reduce-scatter.2.cloned.1.call-start = ((), (), s32[]{:S(2)}) async-start(), calls=%async_computation.4 | async-start | bytes 4325376 | tf_op jit(solution)/shard_map/reduce_scatter | solution.py:87
  316.1 4.3 copy-start.2
  341.7 165.0 %copy-start.3 = (bf16[256,128]{1,0:T(8,128)(2,1)S(1)}, bf16[256,128]{1,0:T(8,128)(2,1)}, u32[]{:S(2)}) copy-start(bf16[256,128]{1,0:T(8,128)(2,1)} %param.12) | copy-start | bytes 196612
  341.7 415.4 %all-reduce.5.cloned.1.call-start = ((), (), s32[]{:S(2)}) async-start(), calls=%async_computation.5 | async-start | bytes 262144 | tf_op jit(solution)/shard_map/psum | solution.py:95
Sparse Core Ops, SparseCore 0:
  11.4 91.0 all-gather.2
  131.6 140.2 all-reduce.2
  274.3 41.6 all-gather.4
  341.8 164.7 reduce-scatter.1
  513.4 243.6 all-reduce.4
where the time goes:
time: 767 us; the launch traced here: 765 us
  waiting for transfers between devices  559 us (73%)
  blocking collectives  119 us (16%)
  other arithmetic  34.9 us (5%)
  local copies, waits for them, and re-layouts  19.6 us (3%)
  matrix products  17.4 us (2%)
  between operations  14.5 us (2%)
    psum x1, waiting for transfers between devices, local(): lax.psum((local_weight, local_bias), ('row', 'col'))  246 us
    psum x1, waiting for transfers between devices, reduce_rows(): lax.psum(partial_value.astype(jnp.bfloat16), 'col').astype(jnp.float32)  140 us
    psum x1, blocking collectives, local(): lax.psum((local_weight, local_bias), ('row', 'col'))  119 us
    all_gather x1, waiting for transfers between devices, local(): lax.all_gather(values.astype(jnp.bfloat16), 'row', axis=0, tiled=True)  92 us
    reduce_scatter x1, waiting for transfers between devices, local(): lax.psum_scatter(backward.astype(jnp.bfloat16), 'row', scatter_dimension=...  45 us
    all_gather x1, waiting for transfers between devices, local(): grad_rows = lax.all_gather(grad_pre, 'col', axis=0, tiled=True)  35.9 us
    scatter-add x2, other arithmetic, step(): return total.at[target].add(contrib)  16.5 us
  transfers between devices with their start and end apart: 5, of which 5 were waited for; matrix products, arithmetic and copies ran while one was open for 1% of the time, Pallas kernels for 0%

commit v1 on v0

v1 whole, which is shorter than its diff:
```python
import functools
import math

import jax
import jax.numpy as jnp
from jax import lax
from jax.experimental import pallas as pl
from jax.experimental.pallas import tpu as pltpu
from jax.sharding import PartitionSpec as P

F32 = jnp.float32
BF16 = jnp.bfloat16
SIDE = 128
UNROLL = 8


def sort_plan(key, other, live, meta, base):
    shape = (SIDE, SIDE)
    lane = lax.broadcasted_iota(jnp.int32, shape, 1)
    sub = lax.broadcasted_iota(jnp.int32, shape, 0)
    key_l = jnp.broadcast_to(jnp.where(live, key, SIDE), shape)
    key_s = key_l.T
    other_s = jnp.broadcast_to(other, shape).T
    less = (key_l < key_s) | ((key_l == key_s) & (lane < sub))
    rank = jnp.sum(less.astype(jnp.int32), axis=1, keepdims=True)
    same = (key_l == key_s) & (lane < sub)
    keep = jnp.minimum(jnp.sum(same.astype(jnp.int32), axis=1, keepdims=True), 1)
    hot = (rank == lane).astype(jnp.int32)
    slot = jnp.sum(hot * sub, axis=0, keepdims=True)
    partner = jnp.sum(hot * other_s, axis=0, keepdims=True)
    kept = jnp.sum(hot * keep, axis=0, keepdims=True)
    upto = jnp.sum((key_s <= lane).astype(jnp.int32), axis=0, keepdims=True)
    here = jnp.sum((key_s == lane).astype(jnp.int32), axis=0, keepdims=True)
    meta[base : base + 1, :] = slot
    meta[base + 1 : base + 2, :] = partner
    meta[base + 2 : base + 3, :] = kept
    meta[base + 3 : base + 4, :] = jnp.maximum(upto - 1, 0)
    meta[base + 4 : base + 5, :] = jnp.minimum(here, 1)


def kernel(
    n_row,
    n_col,
    scale,
    x_ref,
    w_ref,
    b_ref,
    tiles_hbm,
    trow_ref,
    tcol_ref,
    count_ref,
    ct_hbm,
    out_ref,
    gf_ref,
    gw_ref,
    gb_ref,
    panel,
    tiles,
    ct,
    meta_v,
    meta,
    runs,
    rs_send,
    rs_recv,
    grads,
    dw_send,
    dw_recv,
    sib_send,
    sib_recv,
    ring_send,
    ring_recv,
    x_send,
    x_recv,
    d2_send,
    d2_recv,
    d3_send,
    d3_recv,
    local_sem,
    ag_ss,
    ag_rs,
    sib_ss,
    sib_rs,
    col_ss,
    col_rs,
    sr_ss,
    sr_rs,
    ring_ss,
    ring_rs,
    xx_ss,
    xx_rs,
    d2_ss,
    d2_rs,
):
    nz = n_row // 4
    half = nz // 2
    cap = tiles_hbm.shape[0]
    chunk = gw_ref.shape[0] // n_col
    row = lax.axis_index("row")
    col = lax.axis_index("col")
    core = row % 2
    z = (row // 2) % nz
    xh = row // (2 * nz)

    def rid(a, dz, other=0):
        xx = xh if a == 0 else 1 - xh
        kk = core if other == 0 else 1 - core
        return (xx * nz + (z + dz + nz) % nz) * 2 + kk

    def pair(index):
        return pl.ds(2 * index, 2)

    def send(src, dst, ss, rs, to_row=None, to_col=None):
        return pltpu.make_async_remote_copy(
            src_ref=src,
            dst_ref=dst,
            send_sem=ss,
            recv_sem=rs,
            device_id={
                "row": row if to_row is None else to_row,
                "col": col if to_col is None else to_col,
            },
            device_id_type=pl.DeviceIdType.MESH,
        )

    started = []

    def go(copy):
        copy.start()
        started.append(copy)

    sibling = rid(0, 0, 1)
    across = rid(1, 0)
    right = rid(0, 1)
    left = rid(0, -1)
    flips = []
    step = 1
    while step < nz:
        flips.append(rid(0, step * (1 - 2 * ((z // step) % 2))))
        step *= 2
    peers = [(col + j) % n_col for j in range(1, n_col)]

    load_x = pltpu.make_async_copy(x_ref, panel.at[pair(row)], local_sem.at[0])
    load_t = pltpu.make_async_copy(tiles_hbm, tiles, local_sem.at[1])
    load_c = pltpu.make_async_copy(ct_hbm, ct, local_sem.at[2])
    load_x.start()
    load_t.start()
    load_c.start()

    barrier = pltpu.get_barrier_semaphore()
    greet = [sibling, across, right, left] + flips[1:]
    for other in greet:
        pl.semaphore_signal(
            barrier, inc=1, device_id={"row": other, "col": col},
            device_id_type=pl.DeviceIdType.MESH,
        )
    for other in peers:
        pl.semaphore_signal(
            barrier, inc=1, device_id={"row": row, "col": other},
            device_id_type=pl.DeviceIdType.MESH,
        )
    pl.semaphore_wait(barrier, len(greet) + len(peers))

    def ag(src, blk, part, kind, to):
        dst = panel.at[pair(blk)] if part is None else panel.at[pl.ds(2 * blk + part, 1)]
        return send(src, dst, ag_ss.at[kind], ag_rs.at[kind], to)

    def kind(way, a, d):
        return 1 + (way * 2 + a) * half + d - 1

    def part_of(way, d):
        return None if d < half else way

    def view(blk, part):
        return panel.at[pair(blk)] if part is None else panel.at[pl.ds(2 * blk + part, 1)]

    def to_sibling(src, a, dz):
        k = a * nz + dz % nz
        return send(src, panel.at[pair(rid(a, dz))], sib_ss.at[k], sib_rs.at[k], sibling)

    go(ag(x_ref, row, None, kind(0, 0, 1), right))
    go(ag(x_ref, row, None, kind(1, 0, 1), left))
    go(ag(x_ref, row, None, 0, across))
    go(to_sibling(x_ref, 0, 0))

    lane1 = lax.broadcasted_iota(jnp.int32, (1, SIDE), 1)
    live = lane1 < count_ref[0, 0]
    sort_plan(trow_ref[...], tcol_ref[...], live, meta_v, 0)
    sort_plan(tcol_ref[...], trow_ref[...], live, meta_v, 5)
    load_m = pltpu.make_async_copy(meta_v, meta, local_sem.at[3])
    load_m.start()

    blk = rid(1, 0)
    ag(panel.at[pair(blk)], blk, None, 0, across).wait_recv()
    go(ag(panel.at[pair(blk)], blk, None, kind(0, 1, 1), right))
    go(ag(panel.at[pair(blk)], blk, None, kind(1, 1, 1), left))
    go(to_sibling(panel.at[pair(blk)], 1, 0))
    for d in range(1, half + 1):
        for a in (0, 1):
            for way in (0, 1):
                blk = rid(a, -d if way == 0 else d)
                part = part_of(way, d)
                ag(view(blk, part), blk, part, kind(way, a, d), left).wait_recv()
                if d < half:
                    part = part_of(way, d + 1)
                    onward = right if way == 0 else left
                    go(ag(view(blk, part), blk, part, kind(way, a, d + 1), onward))
                    go(to_sibling(panel.at[pair(blk)], a, -d if way == 0 else d))
                elif way == 1:
                    go(to_sibling(panel.at[pair(blk)], a, d))
    for dz in [0] + [s * d for d in range(1, half) for s in (1, -1)] + [half]:
        for a in (0, 1):
            k = a * nz + dz % nz
            dst = panel.at[pair(rid(a, dz, 1))]
            send(dst, dst, sib_ss.at[k], sib_rs.at[k], sibling).wait_recv()
    load_x.wait()
    load_t.wait()
    load_m.wait()

    def products(base, forward):
        def turn(i, acc):
            for u in range(UNROLL):
                s = i * UNROLL + u
                tile = tiles[meta[base, s]]
                if forward:
                    prod = jnp.dot(tile, panel[meta[base + 1, s]], preferred_element_type=F32)
                else:
                    prod = jnp.dot(grads[meta[base + 1, s]], tile, preferred_element_type=F32)
                acc = acc * meta[base + 2, s].astype(F32) + prod
                runs[s] = acc
            return acc

        lax.fori_loop(0, cap // UNROLL, turn, jnp.zeros((SIDE, SIDE), F32))

    def total(base, index):
        return runs[meta[base + 3, index]] * meta[base + 4, index].astype(F32)

    products(0, True)

    for j in range(1, n_col):
        to = peers[j - 1]
        for t in (0, 1):
            rs_send[2 * to + t] = total(0, 2 * to + t).astype(BF16)
        go(send(rs_send.at[pair(to)], rs_recv.at[pair(col)], col_ss.at[j], col_rs.at[j], None, to))
    agg = [total(0, 2 * col + t) for t in (0, 1)]
    load_c.wait()
    for j in range(1, n_col):
        src = (col - j + n_col) % n_col
        send(rs_send.at[pair(src)], rs_recv.at[pair(src)], col_ss.at[j], col_rs.at[j], None, src).wait_recv()
        for t in (0, 1):
            agg[t] = agg[t] + rs_recv[2 * src + t].astype(F32)

    w = w_ref[...]
    gps = []
    outs = []
    for t in (0, 1):
        hi = agg[t].astype(BF16)
        lo = (agg[t] - hi.astype(F32)).astype(BF16)
        pre = jnp.dot(hi, w, preferred_element_type=F32) + jnp.dot(lo, w, preferred_element_type=F32)
        pre = pre + b_ref[...]
        sig = jax.nn.sigmoid(pre)
        outs.append((pre * sig).astype(BF16))
        slope = sig * (1.0 + pre * (1.0 - sig))
        gp = (ct[t * SIDE : (t + 1) * SIDE, :].astype(F32) * slope).astype(BF16)
        gps.append(gp)
        back = lax.dot_general(w, gp, (((1,), (1,)), ((), ())), preferred_element_type=F32)
        grads[2 * col + t] = back.astype(BF16)
    for j in range(1, n_col):
        k = n_col + j
        go(send(grads.at[pair(col)], grads.at[pair(col)], col_ss.at[k], col_rs.at[k], None, peers[j - 1]))

    for t in (0, 1):
        out_ref[t * SIDE : (t + 1) * SIDE, :] = outs[t]
    bias = jnp.sum(gps[0].astype(F32), axis=0, keepdims=True) + jnp.sum(gps[1].astype(F32), axis=0, keepdims=True)
    dw = jnp.zeros(gw_ref.shape, F32)
    for t in (0, 1):
        turned = agg[t].T
        hi = turned.astype(BF16)
        lo = (turned - hi.astype(F32)).astype(BF16)
        dw = dw + jnp.dot(hi, gps[t], preferred_element_type=F32)
        dw = dw + jnp.dot(lo, gps[t], preferred_element_type=F32)
    bias8 = jnp.broadcast_to(bias, (8, bias.shape[1]))
    for c in range(n_col):
        dw_send[c, :chunk, :] = dw[c * chunk : (c + 1) * chunk, :]
        dw_send[c, chunk:, :] = bias8
    dw_recv[col] = dw_send[col]
    for j in range(1, n_col):
        k = 2 * n_col + j
        to = peers[j - 1]
        go(send(dw_send.at[to], dw_recv.at[col], col_ss.at[k], col_rs.at[k], None, to))

    for j in range(1, n_col):
        k = n_col + j
        src = (col - j + n_col) % n_col
        send(grads.at[pair(src)], grads.at[pair(src)], col_ss.at[k], col_rs.at[k], None, src).wait_recv()

    products(5, False)

    order = [half] + [s * d for d in range(half - 1, 0, -1) for s in (1, -1)] + [0]
    for dz in order:
        slot = dz % nz
        for a in (1, 0):
            for t in (0, 1):
                sib_send[slot, 2 * a + t] = total(5, 2 * rid(a, dz, 1) + t).astype(BF16)
        go(send(sib_send.at[slot], sib_recv.at[slot], sr_ss.at[slot], sr_rs.at[slot], sibling))

    for j in range(1, n_col):
        k = 2 * n_col + j
        src = (col - j + n_col) % n_col
        send(dw_send.at[src], dw_recv.at[src], col_ss.at[k], col_rs.at[k], None, src).wait_recv()
    d2_partners = [sibling] + flips + [across]
    weight_sum = [dw_recv[0]]
    for c in range(1, n_col):
        weight_sum[0] = weight_sum[0] + dw_recv[c]

    def d2_copy(i):
        return send(d2_send.at[i], d2_recv.at[i], d2_ss.at[i], d2_rs.at[i], d2_partners[i])

    def d2_start(i):
        d2_send[i] = weight_sum[0]
        go(d2_copy(i))

    def d2_finish(i):
        d2_copy(i).wait_recv()
        weight_sum[0] = d2_send[i] + d2_recv[i]

    d2_start(0)

    def comb(dz, a, t):
        return total(5, 2 * rid(a, dz) + t) + sib_recv[dz % nz, 2 * a + t].astype(F32)

    def sib_wait(dz):
        slot = dz % nz
        send(sib_send.at[slot], sib_recv.at[slot], sr_ss.at[slot], sr_rs.at[slot], sibling).wait_recv()

    def ring(way, n, a):
        k = (way * half + n) * 2 + a
        if n == 0:
            src, dst = ring_send.at[k, pl.ds(way, 1)], ring_recv.at[k, pl.ds(way, 1)]
        else:
            src, dst = ring_send.at[k], ring_recv.at[k]
        return send(src, dst, ring_ss.at[k], ring_rs.at[k], right if way == 0 else left)

    def arrived(way, n, a, t):
        return ring_recv[(way * half + n) * 2 + a, t].astype(F32)

    for n in range(half):
        dist = half - n
        for a in (1, 0):
            for way in (0, 1):
                dz = dist if way == 0 else -dist
                if a == 1 and not (n == 0 and way == 1):
                    sib_wait(dz)
                if n > 0:
                    ring(way, n - 1, a).wait_recv()
                for t in (0, 1):
                    if n == 0 and t != way:
                        continue
                    value = comb(dz, a, t)
                    if n > 1 or (n == 1 and t == way):
                        value = value + arrived(way, n - 1, a, t)
                    ring_send[(way * half + n) * 2 + a, t] = value.astype(BF16)
                go(ring(way, n, a))
        if n < len(d2_partners) - 1:
            d2_finish(n)
            d2_start(n + 1)
    for i in range(half, len(d2_partners) - 1):
        d2_finish(i)
        d2_start(i + 1)
    sib_wait(0)
    last = half - 1
    x_copy = send(x_send, x_recv, xx_ss.at[0], xx_rs.at[0], across)
    done = []
    for a in (1, 0):
        for way in (0, 1):
            ring(way, last, a).wait_recv()
        for t in (0, 1):
            value = comb(0, a, t)
            for way in (0, 1):
                if last > 0 or t == way:
                    value = value + arrived(way, last, a, t)
            if a == 1:
                x_send[t] = value.astype(BF16)
            else:
                done.append(value)
        if a == 1:
            go(x_copy)
    d2_finish(len(d2_partners) - 1)
    d3_send[...] = weight_sum[0][:chunk, :] * scale
    gb_ref[...] = weight_sum[0][chunk : chunk + 1, :] * scale
    d3_recv[col] = d3_send[...]
    for j in range(1, n_col):
        k = 3 * n_col + j
        go(send(d3_send, d3_recv.at[col], col_ss.at[k], col_rs.at[k], None, peers[j - 1]))
    x_copy.wait_recv()
    for t in (0, 1):
        value = done[t] + x_recv[t].astype(F32)
        gf_ref[t * SIDE : (t + 1) * SIDE, :] = value.T.astype(BF16)
    for j in range(1, n_col):
        k = 3 * n_col + j
        src = (col - j + n_col) % n_col
        send(d3_send, d3_recv.at[src], col_ss.at[k], col_rs.at[k], None, src).wait_recv()
    for c in range(n_col):
        gw_ref[c * chunk : (c + 1) * chunk, :] = d3_recv[c]
    for copy in started:
        copy.wait_send()


def local(n_row, n_col, features, weight, bias, tile_values, tile_row, tile_col, tile_count, cotangent):
    nodes, f = features.shape
    h = weight.shape[1]
    cap = tile_values.shape[2]
    nz = n_row // 4
    half = nz // 2
    flips = max(1, nz.bit_length() - 1)
    chunk = f // n_col
    scale = (n_row * n_col * nodes) ** (-0.5)
    pad = SIDE - tile_row.shape[-1]
    trow = jnp.pad(tile_row.reshape(1, -1), ((0, 0), (0, pad)))
    tcol = jnp.pad(tile_col.reshape(1, -1), ((0, 0), (0, pad)))
    vmem = pl.BlockSpec(memory_space=pltpu.VMEM)
    anywhere = pl.BlockSpec(memory_space=pl.ANY)
    dma = pltpu.SemaphoreType.DMA
    square = (SIDE, SIDE)
    output, gf, gw, gb = pl.pallas_call(
        functools.partial(kernel, n_row, n_col, scale),
        out_shape=(
            jax.ShapeDtypeStruct((nodes, h), BF16),
            jax.ShapeDtypeStruct((nodes, f), BF16),
            jax.ShapeDtypeStruct((f, h), F32),
            jax.ShapeDtypeStruct((1, h), F32),
        ),
        in_specs=[anywhere, vmem, vmem, anywhere, vmem, vmem, pl.BlockSpec(memory_space=pltpu.SMEM), anywhere],
        out_specs=(vmem,) * 4,
        scratch_shapes=[
            pltpu.VMEM((2 * n_row,) + square, BF16),
            pltpu.VMEM((cap,) + square, BF16),
            pltpu.VMEM((nodes, h), BF16),
            pltpu.VMEM((16, SIDE), jnp.int32),
            pltpu.SMEM((16, SIDE), jnp.int32),
            pltpu.VMEM((cap,) + square, F32),
            pltpu.VMEM((2 * n_col,) + square, BF16),
            pltpu.VMEM((2 * n_col,) + square, BF16),
            pltpu.VMEM((2 * n_col,) + square, BF16),
            pltpu.VMEM((n_col, chunk + 8, h), F32),
            pltpu.VMEM((n_col, chunk + 8, h), F32),
            pltpu.VMEM((nz, 4) + square, BF16),
            pltpu.VMEM((nz, 4) + square, BF16),
            pltpu.VMEM((4 * half, 2) + square, BF16),
            pltpu.VMEM((4 * half, 2) + square, BF16),
            pltpu.VMEM((2,) + square, BF16),
            pltpu.VMEM((2,) + square, BF16),
            pltpu.VMEM((flips + 2, chunk + 8, h), F32),
            pltpu.VMEM((flips + 2, chunk + 8, h), F32),
            pltpu.VMEM((chunk, h), F32),
            pltpu.VMEM((n_col, chunk, h), F32),
            dma((4,)),
            dma((1 + 4 * half,)),
            dma((1 + 4 * half,)),
            dma((2 * nz,)),
            dma((2 * nz,)),
            dma((4 * n_col,)),
            dma((4 * n_col,)),
            dma((nz,)),
            dma((nz,)),
            dma((4 * half,)),
            dma((4 * half,)),
            dma((1,)),
            dma((1,)),
            dma((flips + 2,)),
            dma((flips + 2,)),
        ],
        compiler_params=pltpu.CompilerParams(
            collective_id=0, has_side_effects=True, vmem_limit_bytes=48 * 1024 * 1024
        ),
    )(
        features.reshape(2, SIDE, f),
        weight,
        bias.reshape(1, h),
        tile_values.reshape(tile_values.shape[2:]),
        trow,
        tcol,
        tile_count,
        cotangent,
    )
    return output, gf, gw, gb.reshape(h)


def solution(mesh):
    placed = (
        P(("col", "row"), None),
        P(),
        P(),
        P("row", "col", None, None, None),
        P("row", "col", None),
        P("row", "col", None),
        P("row", "col"),
        P(("row", "col"), None),
    )
    return jax.shard_map(
        functools.partial(local, mesh.shape["row"], mesh.shape["col"]),
        mesh=mesh,
        in_specs=placed,
        out_specs=(P(("row", "col"), None), P(("col", "row"), None), P(), P()),
        check_vma=False,
    )
```

time: 767 us -> 90.4 us (0.12)
  waiting for transfers between devices: 559 us -> 0 us
  blocking collectives: 119 us -> 0 us
  Pallas kernels: 0 us -> 78.7 us
  other arithmetic: 34.9 us -> 0 us
  matrix products: 17.4 us -> 0 us
  between operations: 14.5 us -> 1.3 us
  local copies, waits for them, and re-layouts: 19.6 us -> 9.25 us
    psum x2 -> x0, waiting for transfers between devices: 386 us -> none  [the longest x1 246 us: local(): lax.psum((local_weight, local_bias), ('row', 'col'))]
    all_gather x2 -> x0, waiting for transfers between devices: 128 us -> none  [the longest x1 92 us: local(): lax.all_gather(values.astype(jnp.bfloat16), 'row', axis=0, tiled=True)]
    psum x1 -> x0, blocking collectives: 119 us -> none  [local(): lax.psum((local_weight, local_bias), ('row', 'col'))]
    pallas_call x0 -> x1, Pallas kernels: none -> 78.7 us  [local(): pl.pallas_call(functools.partial(kernel, n_row, n_col, scale), out_shape=...]
    reduce_scatter x1 -> x0, waiting for transfers between devices: 45 us -> none  [local(): lax.psum_scatter(backward.astype(jnp.bfloat16), 'row', scatter_dimension=...]
    dot_general x7 -> x0, matrix products: 17.4 us -> none  [the longest x1 3.89 us: step(): jnp.einsum('kij,kjh->kih', values_here, lower, preferred_element_type=jnp...]
    scatter-add x2 -> x0, other arithmetic: 16.5 us -> none  [step(): return total.at[target].add(contrib)]
  transfers between devices with their start and end apart: 5 -> 0, of which waited for: 5 -> 0; matrix products, arithmetic and copies ran while one was open for 1% -> 0% of each run, Pallas kernels for 0% -> 0%
where the time goes in v1:
time: 90.4 us; the launch traced here: 89.2 us
  Pallas kernels  78.7 us (87%)
  local copies, waits for them, and re-layouts  9.25 us (10%)
  between operations  1.3 us (1%)
    pallas_call x1, Pallas kernels, local(): pl.pallas_call(functools.partial(kernel, n_row, n_col, scale), out_shape=...  78.7 us
    unnamed x18, local copies, waits for them, and re-layouts  9.25 us

profile of v1, /device:TPU:1, one launch (start us, length us, event | category | flops | bytes accessed | tf_op | source)
XLA Modules:
  0.0 89.2 jit_solution(6170870932906746635)
XLA Ops:
  1.3 0.0 copy-start
  1.3 2.2 %copy-done = bf16[1,1,128,128,128]{4,3,2,1,0:T(8,128)(2,1)S(1)} copy-done((bf16[1,1,128,128,128]{4,3,2,1,0:T(8,128)(2,1)S(1)}, bf16[1,1,128,128,128]{4,3,2,1,0:T(8,128)(2,1)}, u32[]{:S(2)}) %copy-start) | copy-done | bytes 4194328
  3.5 0.0 copy-start.1
  3.5 0.9 %copy-done.1 = bf16[256,256]{1,0:T(8,128)(2,1)S(1)} copy-done((bf16[256,256]{1,0:T(8,128)(2,1)S(1)}, bf16[256,256]{1,0:T(8,128)(2,1)}, u32[]{:S(2)}) %copy-start.1) | copy-done | bytes 131096
  4.4 0.0 copy-start.2
  4.4 0.8 copy-done.2
  5.2 0.0 copy-start.3
  5.2 0.8 copy-done.3
  6.1 0.0 copy-start.4
  6.1 0.7 copy-done.4
  6.7 0.0 copy-start.5
  6.7 0.7 copy-done.5
  7.4 0.0 copy-start.6
  7.4 0.7 copy-done.6
  8.0 78.7 %shard_map.111 = (bf16[256,256]{1,0:T(8,128)(2,1)S(1)}, bf16[256,128]{1,0:T(8,128)(2,1)S(1)}, f32[128,256]{1,0:T(8,128)S(1)}, f32[1,256]{1,0:T(1,128)S(1)}) custom-call(bf16[2,128,128]{2,1,0:T(8,128)(2,1)S(1)} %bitcast.7, bf16[128,256]{1,0:T(8,128)(2,1)S(1)} %copy-done.3, f32[1,256]{1,0:T(1,128)S(1)} %bitcast.8, bf16[128,128,128]{2,1,0:T(8,128)(2,1)S(1)} %bitcast.6, ...), custom_call_target="tpu_custom_call" | custom-call | tf_op jit(solution)/shard_map/pallas_call | solution.py:424
  86.7 0.7 copy.17
  87.4 0.6 copy.18
  88.0 0.7 copy.19
  88.6 0.6 copy.20
Async XLA Ops:
  1.3 2.2 %copy-start = (bf16[1,1,128,128,128]{4,3,2,1,0:T(8,128)(2,1)S(1)}, bf16[1,1,128,128,128]{4,3,2,1,0:T(8,128)(2,1)}, u32[]{:S(2)}) copy-start(bf16[1,1,128,128,128]{4,3,2,1,0:T(8,128)(2,1)} %param.11) | copy-start | bytes 12582916
  3.5 0.9 %copy-start.1 = (bf16[256,256]{1,0:T(8,128)(2,1)S(1)}, bf16[256,256]{1,0:T(8,128)(2,1)}, u32[]{:S(2)}) copy-start(bf16[256,256]{1,0:T(8,128)(2,1)} %ct_hbm.1) | copy-start | bytes 393220
  4.4 0.8 copy-start.2
  5.2 0.8 copy-start.3
  6.1 0.7 copy-start.4
  6.7 0.7 copy-start.5
  7.4 0.7 copy-start.6

commit v2 on v1

v2 whole, which is shorter than its diff:
```python
import functools

import jax
import jax.numpy as jnp
from jax import lax
from jax.experimental import pallas as pl
from jax.experimental.pallas import tpu as pltpu
from jax.sharding import PartitionSpec as P

F32 = jnp.float32
BF16 = jnp.bfloat16
SIDE = 128
UNROLL = 8


def sort_plan(key, other, live, meta, base):
    shape = (SIDE, SIDE)
    lane = lax.broadcasted_iota(jnp.int32, shape, 1)
    sub = lax.broadcasted_iota(jnp.int32, shape, 0)
    key_l = jnp.broadcast_to(jnp.where(live, key, SIDE), shape)
    key_s = key_l.T
    other_s = jnp.broadcast_to(other, shape).T
    less = (key_l < key_s) | ((key_l == key_s) & (lane < sub))
    rank = jnp.sum(less.astype(jnp.int32), axis=1, keepdims=True)
    same = (key_l == key_s) & (lane < sub)
    keep = jnp.minimum(jnp.sum(same.astype(jnp.int32), axis=1, keepdims=True), 1)
    hot = (rank == lane).astype(jnp.int32)
    slot = jnp.sum(hot * sub, axis=0, keepdims=True)
    partner = jnp.sum(hot * other_s, axis=0, keepdims=True)
    kept = jnp.sum(hot * keep, axis=0, keepdims=True)
    upto = jnp.sum((key_s <= lane).astype(jnp.int32), axis=0, keepdims=True)
    here = jnp.sum((key_s == lane).astype(jnp.int32), axis=0, keepdims=True)
    meta[base : base + 1, :] = slot
    meta[base + 1 : base + 2, :] = partner
    meta[base + 2 : base + 3, :] = kept
    meta[base + 3 : base + 4, :] = jnp.maximum(upto - 1, 0)
    meta[base + 4 : base + 5, :] = jnp.minimum(here, 1)


def kernel(
    n_row,
    n_col,
    scale,
    x_ref,
    w_hbm,
    b_hbm,
    tiles_hbm,
    trow_hbm,
    tcol_hbm,
    count_ref,
    ct_hbm,
    out_ref,
    gf_ref,
    gw_ref,
    gb_ref,
    w_ref,
    b_ref,
    trow_ref,
    tcol_ref,
    panel,
    tiles,
    ct,
    meta_v,
    meta,
    runs,
    rs_send,
    rs_recv,
    grads,
    sib_send,
    sib_recv,
    ring_send,
    ring_recv,
    wz_send,
    wz_recv,
    wc_send,
    wc_recv,
    wx_send,
    wx_recv,
    wg_send,
    wg_recv,
    local_sem,
    ag_ss,
    ag_rs,
    sib_ss,
    sib_rs,
    col_ss,
    col_rs,
    sr_ss,
    sr_rs,
    ring_ss,
    ring_rs,
    w_ss,
    w_rs,
):
    nz = n_row // 4
    ny = n_col // 2
    cap = tiles_hbm.shape[0]
    chunk = gw_ref.shape[0] // nz
    row = lax.axis_index("row")
    col = lax.axis_index("col")
    core = row % 2
    z = (row // 2) % nz
    xh = row // (2 * nz)
    y = col // 2
    xl = col % 2

    def rid(a, dz, other=0):
        xx = xh if a == 0 else 1 - xh
        kk = core if other == 0 else 1 - core
        return (xx * nz + (z + dz + nz) % nz) * 2 + kk

    def cid(dy, dx):
        return ((y + dy + ny) % ny) * 2 + (xl + dx) % 2

    def pair(index):
        return pl.ds(2 * index, 2)

    def send(src, dst, ss, rs, to_row=None, to_col=None):
        return pltpu.make_async_remote_copy(
            src_ref=src,
            dst_ref=dst,
            send_sem=ss,
            recv_sem=rs,
            device_id={
                "row": row if to_row is None else to_row,
                "col": col if to_col is None else to_col,
            },
            device_id_type=pl.DeviceIdType.MESH,
        )

    started = []

    def go(copy):
        copy.start()
        started.append(copy)

    sibling = rid(0, 0, 1)
    across = rid(1, 0)
    shifts = sorted(
        ((dy, dx) for dy in range(ny) for dx in range(2) if dy or dx),
        key=lambda p: -(min(p[0], ny - p[0]) + p[1]),
    )

    loads = [
        pltpu.make_async_copy(src, dst, local_sem.at[i])
        for i, (src, dst) in enumerate(
            (
                (trow_hbm, trow_ref),
                (tcol_hbm, tcol_ref),
                (x_ref, panel.at[pair(row)]),
                (w_hbm, w_ref),
                (b_hbm, b_ref),
                (ct_hbm, ct),
                (tiles_hbm, tiles),
            )
        )
    ]
    for load in loads:
        load.start()

    barrier = pltpu.get_barrier_semaphore()
    greet = [sibling, across, rid(1, 0, 1)] + [rid(0, d) for d in range(1, nz)]
    for other in greet:
        pl.semaphore_signal(
            barrier, inc=1, device_id={"row": other, "col": col},
            device_id_type=pl.DeviceIdType.MESH,
        )
    for shift in shifts:
        pl.semaphore_signal(
            barrier, inc=1, device_id={"row": row, "col": cid(*shift)},
            device_id_type=pl.DeviceIdType.MESH,
        )
    pl.semaphore_wait(barrier, len(greet) + len(shifts))

    def ag(a, dz, t, to, src=None):
        k = (a * nz + dz % nz) * 2 + t
        if src is None:
            src = rid(a, dz)
        return send(
            x_ref.at[pl.ds(t, 1)] if to is not None and src is row else panel.at[pl.ds(2 * src + t, 1)],
            panel.at[pl.ds(2 * src + t, 1)],
            ag_ss.at[k],
            ag_rs.at[k],
            across if to is None else to,
        )

    def ag_wait(a, dz, t):
        ag(a, dz, t, None).wait_recv()

    def to_sibling(a, dz):
        k = a * nz + dz % nz
        blk = rid(a, dz)
        src = x_ref if a == 0 and dz == 0 else panel.at[pair(blk)]
        go(send(src, panel.at[pair(blk)], sib_ss.at[k], sib_rs.at[k], sibling))

    signs = (1, -1)
    for t in (0, 1):
        for e in signs:
            go(ag(0, -2 * e, t, rid(0, 2 * e), row))
        go(ag(1, 0, t, across, row))
    for t in (0, 1):
        for e in signs:
            go(ag(0, -e, t, rid(0, e), row))
    to_sibling(0, 0)

    for load in loads[:2]:
        load.wait()
    lane1 = lax.broadcasted_iota(jnp.int32, (1, SIDE), 1)
    live = lane1 < count_ref[0, 0]
    sort_plan(trow_ref[...], tcol_ref[...], live, meta_v, 0)
    sort_plan(tcol_ref[...], trow_ref[...], live, meta_v, 5)
    load_m = pltpu.make_async_copy(meta_v, meta, local_sem.at[7])
    load_m.start()

    for t in (0, 1):
        for e in signs:
            ag_wait(0, -2 * e, t)
            go(ag(1, -2 * e, t, across, rid(0, -2 * e)))
    for t in (0, 1):
        ag_wait(1, 0, t)
        for e in signs:
            go(ag(0, -3 * e, t, rid(0, e), rid(0, -2 * e)))
            go(ag(1, -e, t, rid(0, e), across))
    for t, e in enumerate(signs):
        go(ag(0, 4, t, rid(0, 2 * e), rid(0, -2 * e)))
    for e in signs:
        to_sibling(0, -2 * e)
    to_sibling(1, 0)
    for e in signs:
        for t in (0, 1):
            ag_wait(0, -e, t)
        to_sibling(0, -e)
    for t in (0, 1):
        for e in signs:
            ag_wait(1, -2 * e, t)
            if t == (0 if e == 1 else 1):
                go(ag(1, 4, t, rid(0, 2 * e), rid(1, -2 * e)))
            go(ag(1, -3 * e, t, rid(0, e), rid(1, -2 * e)))
    for e in signs:
        to_sibling(1, -2 * e)
    for a, dz in ((0, -3), (0, 3), (1, -1), (1, 1), (0, 4), (1, -3), (1, 3), (1, 4)):
        for t in (0, 1):
            ag_wait(a, dz, t)
        to_sibling(a, dz)
    for dz in (0, -2, 2, -1, 1, -3, 3, 4):
        for a in (0, 1):
            k = a * nz + dz % nz
            dst = panel.at[pair(rid(a, dz, 1))]
            send(dst, dst, sib_ss.at[k], sib_rs.at[k], sibling).wait_recv()
    for load in loads[2:]:
        load.wait()
    load_m.wait()

    def products(base, forward):
        def turn(i, acc):
            for u in range(UNROLL):
                s = i * UNROLL + u
                tile = tiles[meta[base, s]]
                if forward:
                    prod = jnp.dot(tile, panel[meta[base + 1, s]], preferred_element_type=F32)
                else:
                    prod = jnp.dot(grads[meta[base + 1, s]], tile, preferred_element_type=F32)
                acc = acc * meta[base + 2, s].astype(F32) + prod
                runs[s] = acc
            return acc

        lax.fori_loop(0, cap // UNROLL, turn, jnp.zeros((SIDE, SIDE), F32))

    def total(base, index):
        return runs[meta[base + 3, index]] * meta[base + 4, index].astype(F32)

    products(0, True)

    def cc(src, dst, k, to):
        return send(src, dst, col_ss.at[k], col_rs.at[k], None, to)

    for j, shift in enumerate(shifts):
        to = cid(*shift)
        for t in (0, 1):
            rs_send[2 * to + t] = total(0, 2 * to + t).astype(BF16)
        go(cc(rs_send.at[pair(to)], rs_recv.at[pair(col)], j, to))
    agg = [total(0, 2 * col + t) for t in (0, 1)]
    for j, (dy, dx) in reversed(list(enumerate(shifts))):
        src = cid(-dy, dx)
        cc(rs_send.at[pair(src)], rs_recv.at[pair(src)], j, src).wait_recv()
        for t in (0, 1):
            agg[t] = agg[t] + rs_recv[2 * src + t].astype(F32)

    w = w_ref[...]
    gps = []
    outs = []
    for t in (0, 1):
        hi = agg[t].astype(BF16)
        lo = (agg[t] - hi.astype(F32)).astype(BF16)
        pre = jnp.dot(hi, w, preferred_element_type=F32) + jnp.dot(lo, w, preferred_element_type=F32)
        pre = pre + b_ref[...]
        sig = jax.nn.sigmoid(pre)
        outs.append((pre * sig).astype(BF16))
        slope = sig * (1.0 + pre * (1.0 - sig))
        gp = (ct[t * SIDE : (t + 1) * SIDE, :].astype(F32) * slope).astype(BF16)
        gps.append(gp)
        back = lax.dot_general(w, gp, (((1,), (1,)), ((), ())), preferred_element_type=F32)
        grads[2 * col + t] = back.astype(BF16)
        own = grads.at[pl.ds(2 * col + t, 1)]
        for j, shift in enumerate(shifts):
            go(cc(own, own, (1 + t) * n_col + j, cid(*shift)))

    bias = jnp.sum(gps[0].astype(F32), axis=0, keepdims=True) + jnp.sum(gps[1].astype(F32), axis=0, keepdims=True)
    dw = jnp.zeros(gw_ref.shape, F32)
    for t in (0, 1):
        turned = agg[t].T
        hi = turned.astype(BF16)
        lo = (turned - hi.astype(F32)).astype(BF16)
        dw = dw + jnp.dot(hi, gps[t], preferred_element_type=F32)
        dw = dw + jnp.dot(lo, gps[t], preferred_element_type=F32)
    bias8 = jnp.broadcast_to(bias, (8, bias.shape[1]))
    for c in range(nz):
        wz_send[c, :chunk, :] = dw[c * chunk : (c + 1) * chunk, :]
        wz_send[c, chunk:, :] = bias8
    wz_recv[z] = wz_send[z]

    def wcopy(src, dst, k, to_row=None, to_col=None):
        return send(src, dst, w_ss.at[k], w_rs.at[k], to_row, to_col)

    far = sorted(range(1, nz), key=lambda d: -min(d, nz - d))
    for d in far:
        go(wcopy(wz_send.at[(z + d) % nz], wz_recv.at[z], d, rid(0, d)))
    for t in (0, 1):
        out_ref[t * SIDE : (t + 1) * SIDE, :] = outs[t]

    for t in (0, 1):
        for j, (dy, dx) in enumerate(shifts):
            src = cid(-dy, dx)
            there = grads.at[pl.ds(2 * src + t, 1)]
            cc(there, there, (1 + t) * n_col + j, src).wait_recv()

    products(5, False)

    def added(ref, n):
        value = ref[0]
        for i in range(1, n):
            value = value + ref[i]
        return value

    def over_z_done():
        for d in far:
            src = (z - d + nz) % nz
            wcopy(wz_send.at[src], wz_recv.at[src], d, rid(0, -d)).wait_recv()
        value = added(wz_recv, nz)
        wc_send[...] = value
        wc_recv[col] = value
        for j, shift in enumerate(shifts):
            go(wcopy(wc_send, wc_recv.at[col], nz + j, None, cid(*shift)))

    quad = 2 * xh + core
    quads = ((1, 1), (1, 0), (0, 1))

    def over_col_done():
        for j, (dy, dx) in enumerate(shifts):
            src = cid(-dy, dx)
            wcopy(wc_send, wc_recv.at[src], nz + j, None, src).wait_recv()
        value = added(wc_recv, n_col)
        wx_send[...] = value
        wx_recv[quad] = value
        for j, (a, other) in enumerate(quads):
            go(wcopy(wx_send, wx_recv.at[quad], nz + n_col + j, rid(a, 0, other)))

    def over_quad_done():
        for j, (a, other) in enumerate(quads):
            src = 2 * (xh if a == 0 else 1 - xh) + (core if other == 0 else 1 - core)
            wcopy(wx_send, wx_recv.at[src], nz + n_col + j, rid(a, 0, other)).wait_recv()
        value = added(wx_recv, 4) * scale
        gb_ref[...] = value[chunk : chunk + 1, :]
        wg_send[...] = value[:chunk, :]
        wg_recv[z] = value[:chunk, :]
        for d in far:
            go(wcopy(wg_send, wg_recv.at[z], nz + n_col + 4 + d, rid(0, d)))

    def gathered():
        for d in far:
            src = (z - d + nz) % nz
            wcopy(wg_send, wg_recv.at[src], nz + n_col + 4 + d, rid(0, -d)).wait_recv()
        for c in range(nz):
            gw_ref[c * chunk : (c + 1) * chunk, :] = wg_recv[c]

    order = [(1, 3), (1, -3), (1, 4), (0, 3), (0, -3), (0, 4), (1, 2), (1, -2)]
    order += [(1, 1), (1, -1), (0, 1), (0, -1), (0, 2), (0, -2), (1, 0), (0, 0)]

    def sib_copy(a, dz):
        k = a * nz + dz % nz
        return send(sib_send.at[k], sib_recv.at[k], sr_ss.at[k], sr_rs.at[k], sibling)

    for a, dz in order:
        for t in (0, 1):
            sib_send[a * nz + dz % nz, t] = total(5, 2 * rid(a, dz, 1) + t).astype(BF16)
        go(sib_copy(a, dz))
    over_z_done()

    def comb(a, dz, t):
        return total(5, 2 * rid(a, dz) + t) + sib_recv[a * nz + dz % nz, t].astype(F32)

    slots = {}
    for a in (0, 1):
        for e in signs:
            for name in ("three", "four", "one"):
                slots[name, a, e] = len(slots)
    for e in signs:
        slots["cross", 0, e] = len(slots)
        slots["two", 0, e] = len(slots)
    slots["zero", 0, 1] = len(slots)

    def ring(name, a, e, t, to):
        k = slots[name, a, e]
        return send(
            ring_send.at[k, pl.ds(t, 1)],
            ring_recv.at[k, pl.ds(t, 1)],
            ring_ss.at[2 * k + t],
            ring_rs.at[2 * k + t],
            to,
        )

    def ring_go(name, a, e, t, to, value):
        ring_send[slots[name, a, e], t] = value.astype(BF16)
        go(ring(name, a, e, t, to))

    def arrived(name, a, e, t):
        ring(name, a, e, t, across).wait_recv()
        return ring_recv[slots[name, a, e], t].astype(F32)

    for a in (1, 0):
        for e in signs:
            sib_copy(a, 3 * e).wait_recv()
            for t in (0, 1):
                ring_go("three", a, e, t, rid(0, e), comb(a, 3 * e, t))
        sib_copy(a, 4).wait_recv()
        for t, e in enumerate((-1, 1)):
            ring_go("four", a, e, t, rid(0, 2 * e), comb(a, 4, t))
    for a in (1, 0):
        for e in signs:
            sib_copy(a, e).wait_recv()
            for t in (0, 1):
                ring_go("one", a, e, t, rid(0, e), comb(a, e, t))

    def near(a, e, t):
        value = comb(a, 2 * e, t) + arrived("three", a, e, t)
        if t == (0 if e == -1 else 1):
            value = value + arrived("four", a, e, t)
        return value

    for e in signs:
        sib_copy(1, 2 * e).wait_recv()
    for t in (0, 1):
        for e in signs:
            ring_go("cross", 0, e, t, across, near(1, e, t))
    over_col_done()
    sib_copy(1, 0).wait_recv()
    for t in (0, 1):
        value = comb(1, 0, t) + arrived("one", 1, 1, t) + arrived("one", 1, -1, t)
        ring_go("zero", 0, 1, t, across, value)
    for e in signs:
        sib_copy(0, 2 * e).wait_recv()
    for t in (0, 1):
        for e in signs:
            value = near(0, e, t) + arrived("cross", 0, e, t)
            ring_go("two", 0, e, t, rid(0, 2 * e), value)
    over_quad_done()
    sib_copy(0, 0).wait_recv()
    for t in (0, 1):
        value = comb(0, 0, t)
        for e in signs:
            value = value + arrived("one", 0, e, t)
        value = value + arrived("zero", 0, 1, t)
        for e in signs:
            value = value + arrived("two", 0, e, t)
        gf_ref[t * SIDE : (t + 1) * SIDE, :] = value.T.astype(BF16)
    gathered()
    for copy in started:
        copy.wait_send()


def write_out(*refs):
    copies = [pltpu.make_async_copy(refs[i], refs[4 + i], refs[8].at[i]) for i in range(4)]
    for copy in copies:
        copy.start()
    for copy in copies:
        copy.wait()


def local(n_row, n_col, features, weight, bias, tile_values, tile_row, tile_col, tile_count, cotangent):
    nodes, f = features.shape
    h = weight.shape[1]
    cap = tile_values.shape[2]
    nz = n_row // 4
    chunk = f // nz
    scale = (n_row * n_col * nodes) ** (-0.5)
    pad = SIDE - tile_row.shape[-1]
    trow = jnp.pad(tile_row.reshape(1, -1), ((0, 0), (0, pad)))
    tcol = jnp.pad(tile_col.reshape(1, -1), ((0, 0), (0, pad)))
    vmem = pl.BlockSpec(memory_space=pltpu.VMEM)
    hbm = pl.BlockSpec(memory_space=pltpu.HBM)
    dma = pltpu.SemaphoreType.DMA
    square = (SIDE, SIDE)
    output, gf, gw, gb = pl.pallas_call(
        functools.partial(kernel, n_row, n_col, scale),
        out_shape=(
            jax.ShapeDtypeStruct((nodes, h), BF16),
            jax.ShapeDtypeStruct((nodes, f), BF16),
            jax.ShapeDtypeStruct((f, h), F32),
            jax.ShapeDtypeStruct((1, h), F32),
        ),
        in_specs=[hbm] * 6 + [pl.BlockSpec(memory_space=pltpu.SMEM), hbm],
        out_specs=(vmem,) * 4,
        scratch_shapes=[
            pltpu.VMEM((f, h), BF16),
            pltpu.VMEM((1, h), F32),
            pltpu.VMEM((1, SIDE), jnp.int32),
            pltpu.VMEM((1, SIDE), jnp.int32),
            pltpu.VMEM((2 * n_row,) + square, BF16),
            pltpu.VMEM((cap,) + square, BF16),
            pltpu.VMEM((nodes, h), BF16),
            pltpu.VMEM((16, SIDE), jnp.int32),
            pltpu.SMEM((16, SIDE), jnp.int32),
            pltpu.VMEM((cap,) + square, F32),
            pltpu.VMEM((2 * n_col,) + square, BF16),
            pltpu.VMEM((2 * n_col,) + square, BF16),
            pltpu.VMEM((2 * n_col,) + square, BF16),
            pltpu.VMEM((2 * nz, 2) + square, BF16),
            pltpu.VMEM((2 * nz, 2) + square, BF16),
            pltpu.VMEM((17, 2) + square, BF16),
            pltpu.VMEM((17, 2) + square, BF16),
            pltpu.VMEM((nz, chunk + 8, h), F32),
            pltpu.VMEM((nz, chunk + 8, h), F32),
            pltpu.VMEM((chunk + 8, h), F32),
            pltpu.VMEM((n_col, chunk + 8, h), F32),
            pltpu.VMEM((chunk + 8, h), F32),
            pltpu.VMEM((4, chunk + 8, h), F32),
            pltpu.VMEM((chunk, h), F32),
            pltpu.VMEM((nz, chunk, h), F32),
            dma((8,)),
            dma((4 * nz,)),
            dma((4 * nz,)),
            dma((2 * nz,)),
            dma((2 * nz,)),
            dma((3 * n_col,)),
            dma((3 * n_col,)),
            dma((2 * nz,)),
            dma((2 * nz,)),
            dma((34,)),
            dma((34,)),
            dma((2 * nz + n_col + 4,)),
            dma((2 * nz + n_col + 4,)),
        ],
        compiler_params=pltpu.CompilerParams(
            collective_id=0, has_side_effects=True, vmem_limit_bytes=48 * 1024 * 1024
        ),
    )(
        *(
            pltpu.with_memory_space_constraint(operand, pltpu.HBM)
            for operand in (
                features.reshape(2, SIDE, f),
                weight,
                bias.reshape(1, h),
                tile_values.reshape(tile_values.shape[2:]),
                trow,
                tcol,
            )
        ),
        tile_count,
        pltpu.with_memory_space_constraint(cotangent, pltpu.HBM),
    )
    results = (output, gf, gw, gb)
    output, gf, gw, gb = pl.pallas_call(
        write_out,
        out_shape=tuple(jax.ShapeDtypeStruct(a.shape, a.dtype) for a in results),
        in_specs=[pl.BlockSpec(memory_space=pl.ANY)] * 4,
        out_specs=(hbm,) * 4,
        scratch_shapes=[dma((4,))],
        compiler_params=pltpu.CompilerParams(vmem_limit_bytes=1024 * 1024),
    )(*(pltpu.with_memory_space_constraint(a, pltpu.VMEM) for a in results))
    return output, gf, gw, gb.reshape(h)


def solution(mesh):
    placed = (
        P(("col", "row"), None),
        P(),
        P(),
        P("row", "col", None, None, None),
        P("row", "col", None),
        P("row", "col", None),
        P("row", "col"),
        P(("row", "col"), None),
    )
    return jax.shard_map(
        functools.partial(local, mesh.shape["row"], mesh.shape["col"]),
        mesh=mesh,
        in_specs=placed,
        out_specs=(P(("row", "col"), None), P(("col", "row"), None), P(), P()),
        check_vma=False,
    )
```

time: 90.4 us -> 72.6 us (0.80); the launches traced: 89.2 us -> 72.6 us
  local copies, waits for them, and re-layouts: 9.25 us -> 0 us
  Pallas kernels: 78.7 us -> 71.3 us
    unnamed x18 -> x0, local copies, waits for them, and re-layouts: 9.25 us -> none
    pallas_call x1, Pallas kernels: 78.7 us -> 70.5 us  [local(): pl.pallas_call(functools.partial(kernel, n_row, n_col, scale), out_shape=...]
where the time goes in v2:
time: 72.6 us
  Pallas kernels  71.3 us (98%)
  between operations  1.29 us (2%)
    pallas_call x1, Pallas kernels, local(): pl.pallas_call(functools.partial(kernel, n_row, n_col, scale), out_shape=...  70.5 us

profile of v2, /device:TPU:1, one launch (start us, length us, event | category | flops | bytes accessed | tf_op | source)
XLA Modules:
  0.0 72.6 jit_solution(1098550176922334142)
XLA Ops:
  1.3 70.5 %shard_map.111 = (bf16[256,256]{1,0:T(8,128)(2,1)S(1)}, bf16[256,128]{1,0:T(8,128)(2,1)S(1)}, f32[128,256]{1,0:T(8,128)S(1)}, f32[1,256]{1,0:T(1,128)S(1)}) custom-call(bf16[2,128,128]{2,1,0:T(8,128)(2,1)} %bitcast.7, bf16[128,256]{1,0:T(8,128)(2,1)} %w_hbm.1, f32[1,256]{1,0:T(1,128)} %bitcast.8, bf16[128,128,128]{2,1,0:T(8,128)(2,1)} %bitcast.6, ...), custom_call_target="tpu_custom_call" | custom-call | tf_op jit(solution)/shard_map/pallas_call | solution.py:503
  71.8 0.8 %shard_map.112 = (bf16[256,256]{1,0:T(8,128)(2,1)}, bf16[256,128]{1,0:T(8,128)(2,1)}, f32[128,256]{1,0:T(8,128)}, f32[1,256]{1,0:T(1,128)}) custom-call(bf16[256,256]{1,0:T(8,128)(2,1)S(1)} %get-tuple-element.12.refs_0_, bf16[256,128]{1,0:T(8,128)(2,1)S(1)} %get-tuple-element.13.refs_1_, f32[128,256]{1,0:T(8,128)S(1)} %get-tuple-element.14.refs_2_, ...), custom_call_target="tpu_custom_call" | custom-call | tf_op jit(solution)/shard_map/pallas_call | solution.py:572

commit v3 on v2

--- a/solution.py
+++ b/solution.py
@@ -159,7 +159,7 @@
         load.start()
 
     barrier = pltpu.get_barrier_semaphore()
-    greet = [sibling, across, rid(1, 0, 1)] + [rid(0, d) for d in range(1, nz)]
+    greet = [sibling, across] + [rid(0, d) for d in (1, 2, -1, -2)]
     for other in greet:
         pl.semaphore_signal(
             barrier, inc=1, device_id={"row": other, "col": col},
@@ -274,24 +274,27 @@
     def cc(src, dst, k, to):
         return send(src, dst, col_ss.at[k], col_rs.at[k], None, to)
 
-    for j, shift in enumerate(shifts):
-        to = cid(*shift)
-        for t in (0, 1):
-            rs_send[2 * to + t] = total(0, 2 * to + t).astype(BF16)
-        go(cc(rs_send.at[pair(to)], rs_recv.at[pair(col)], j, to))
-    agg = [total(0, 2 * col + t) for t in (0, 1)]
-    for j, (dy, dx) in reversed(list(enumerate(shifts))):
-        src = cid(-dy, dx)
-        cc(rs_send.at[pair(src)], rs_recv.at[pair(src)], j, src).wait_recv()
-        for t in (0, 1):
-            agg[t] = agg[t] + rs_recv[2 * src + t].astype(F32)
+    for t in (0, 1):
+        for j, shift in enumerate(shifts):
+            i = 2 * cid(*shift) + t
+            rs_send[i] = total(0, i).astype(BF16)
+            mine = rs_recv.at[pl.ds(2 * col + t, 1)]
+            go(cc(rs_send.at[pl.ds(i, 1)], mine, t * n_col + j, cid(*shift)))
 
     w = w_ref[...]
+    agg = []
     gps = []
     outs = []
     for t in (0, 1):
-        hi = agg[t].astype(BF16)
-        lo = (agg[t] - hi.astype(F32)).astype(BF16)
+        value = total(0, 2 * col + t)
+        for j, (dy, dx) in reversed(list(enumerate(shifts))):
+            src = cid(-dy, dx)
+            i = 2 * src + t
+            cc(rs_send.at[pl.ds(i, 1)], rs_recv.at[pl.ds(i, 1)], t * n_col + j, src).wait_recv()
+            value = value + rs_recv[i].astype(F32)
+        agg.append(value)
+        hi = value.astype(BF16)
+        lo = (value - hi.astype(F32)).astype(BF16)
         pre = jnp.dot(hi, w, preferred_element_type=F32) + jnp.dot(lo, w, preferred_element_type=F32)
         pre = pre + b_ref[...]
         sig = jax.nn.sigmoid(pre)
@@ -303,7 +306,7 @@
         grads[2 * col + t] = back.astype(BF16)
         own = grads.at[pl.ds(2 * col + t, 1)]
         for j, shift in enumerate(shifts):
-            go(cc(own, own, (1 + t) * n_col + j, cid(*shift)))
+            go(cc(own, own, (2 + t) * n_col + j, cid(*shift)))
 
     bias = jnp.sum(gps[0].astype(F32), axis=0, keepdims=True) + jnp.sum(gps[1].astype(F32), axis=0, keepdims=True)
     dw = jnp.zeros(gw_ref.shape, F32)
@@ -332,7 +335,7 @@
         for j, (dy, dx) in enumerate(shifts):
             src = cid(-dy, dx)
             there = grads.at[pl.ds(2 * src + t, 1)]
-            cc(there, there, (1 + t) * n_col + j, src).wait_recv()
+            cc(there, there, (2 + t) * n_col + j, src).wait_recv()
 
     products(5, False)
 
@@ -541,8 +544,8 @@
             dma((4 * nz,)),
             dma((2 * nz,)),
             dma((2 * nz,)),
-            dma((3 * n_col,)),
-            dma((3 * n_col,)),
+            dma((4 * n_col,)),
+            dma((4 * n_col,)),
             dma((2 * nz,)),
             dma((2 * nz,)),
             dma((34,)),

time: 72.6 us -> 68.8 us (0.948)
  Pallas kernels: 71.3 us -> 67.2 us
    pallas_call x1, Pallas kernels: 70.5 us -> 66.4 us  [local(): pl.pallas_call(functools.partial(kernel, n_row, n_col, scale), out_shape=...]
where the time goes in v3:
time: 68.8 us; the launch traced here: 68.5 us
  Pallas kernels  67.2 us (98%)
  between operations  1.29 us (2%)
    pallas_call x1, Pallas kernels, local(): pl.pallas_call(functools.partial(kernel, n_row, n_col, scale), out_shape=...  66.4 us

profile of v3, /device:TPU:1, one launch (start us, length us, event | category | flops | bytes accessed | tf_op | source)
XLA Modules:
  0.0 68.5 jit_solution(18003448988681297627)
XLA Ops:
  1.3 66.4 %shard_map.111 = (bf16[256,256]{1,0:T(8,128)(2,1)S(1)}, bf16[256,128]{1,0:T(8,128)(2,1)S(1)}, f32[128,256]{1,0:T(8,128)S(1)}, f32[1,256]{1,0:T(1,128)S(1)}) custom-call(bf16[2,128,128]{2,1,0:T(8,128)(2,1)} %bitcast.7, bf16[128,256]{1,0:T(8,128)(2,1)} %w_hbm.1, f32[1,256]{1,0:T(1,128)} %bitcast.8, bf16[128,128,128]{2,1,0:T(8,128)(2,1)} %bitcast.6, ...), custom_call_target="tpu_custom_call" | custom-call | tf_op jit(solution)/shard_map/pallas_call | solution.py:506
  67.7 0.8 %shard_map.112 = (bf16[256,256]{1,0:T(8,128)(2,1)}, bf16[256,128]{1,0:T(8,128)(2,1)}, f32[128,256]{1,0:T(8,128)}, f32[1,256]{1,0:T(1,128)}) custom-call(bf16[256,256]{1,0:T(8,128)(2,1)S(1)} %get-tuple-element.12.refs_0_, bf16[256,128]{1,0:T(8,128)(2,1)S(1)} %get-tuple-element.13.refs_1_, f32[128,256]{1,0:T(8,128)S(1)} %get-tuple-element.14.refs_2_, ...), custom_call_target="tpu_custom_call" | custom-call | tf_op jit(solution)/shard_map/pallas_call | solution.py:575

commit v4 on v3

--- a/solution.py
+++ b/solution.py
@@ -10,7 +10,7 @@
 F32 = jnp.float32
 BF16 = jnp.bfloat16
 SIDE = 128
-UNROLL = 8
+UNROLL = 64
 
 
 def sort_plan(key, other, live, meta, base):
@@ -134,6 +134,11 @@
         copy.start()
         started.append(copy)
 
+    def drain(keep):
+        for copy in started[: len(started) - keep]:
+            copy.wait_send()
+        del started[: len(started) - keep]
+
     sibling = rid(0, 0, 1)
     across = rid(1, 0)
     shifts = sorted(
@@ -281,6 +286,7 @@
             mine = rs_recv.at[pl.ds(2 * col + t, 1)]
             go(cc(rs_send.at[pl.ds(i, 1)], mine, t * n_col + j, cid(*shift)))
 
+    drain(2 * len(shifts))
     w = w_ref[...]
     agg = []
     gps = []
@@ -331,6 +337,7 @@
     for t in (0, 1):
         out_ref[t * SIDE : (t + 1) * SIDE, :] = outs[t]
 
+    drain(2 * len(shifts) + len(far))
     for t in (0, 1):
         for j, (dy, dx) in enumerate(shifts):
             src = cid(-dy, dx)
@@ -444,6 +451,8 @@
             for t in (0, 1):
                 ring_go("one", a, e, t, rid(0, e), comb(a, e, t))
 
+    drain(24)
+
     def near(a, e, t):
         value = comb(a, 2 * e, t) + arrived("three", a, e, t)
         if t == (0 if e == -1 else 1):
@@ -467,6 +476,7 @@
             value = near(0, e, t) + arrived("cross", 0, e, t)
             ring_go("two", 0, e, t, rid(0, 2 * e), value)
     over_quad_done()
+    drain(2 * len(signs) + len(far))
     sib_copy(0, 0).wait_recv()
     for t in (0, 1):
         value = comb(0, 0, t)
@@ -477,8 +487,7 @@
             value = value + arrived("two", 0, e, t)
         gf_ref[t * SIDE : (t + 1) * SIDE, :] = value.T.astype(BF16)
     gathered()
-    for copy in started:
-        copy.wait_send()
+    drain(0)
 
 
 def write_out(*refs):

time: 68.8 us -> 64.6 us (0.939)
  Pallas kernels: 67.2 us -> 62.8 us
    pallas_call x1, Pallas kernels: 66.4 us -> 62 us  [local(): pl.pallas_call(functools.partial(kernel, n_row, n_col, scale), out_shape=...]
where the time goes in v4:
time: 64.6 us; the launch traced here: 64 us
  Pallas kernels  62.8 us (97%)
  between operations  1.29 us (2%)
    pallas_call x1, Pallas kernels, local(): pl.pallas_call(functools.partial(kernel, n_row, n_col, scale), out_shape=...  62 us

profile of v4, /device:TPU:1, one launch (start us, length us, event | category | flops | bytes accessed | tf_op | source)
XLA Modules:
  0.0 64.0 jit_solution(15823840040770628121)
XLA Ops:
  1.3 62.0 %shard_map.111 = (bf16[256,256]{1,0:T(8,128)(2,1)S(1)}, bf16[256,128]{1,0:T(8,128)(2,1)S(1)}, f32[128,256]{1,0:T(8,128)S(1)}, f32[1,256]{1,0:T(1,128)S(1)}) custom-call(bf16[2,128,128]{2,1,0:T(8,128)(2,1)} %bitcast.7, bf16[128,256]{1,0:T(8,128)(2,1)} %w_hbm.1, f32[1,256]{1,0:T(1,128)} %bitcast.8, bf16[128,128,128]{2,1,0:T(8,128)(2,1)} %bitcast.6, ...), custom_call_target="tpu_custom_call" | custom-call | tf_op jit(solution)/shard_map/pallas_call | solution.py:515
  63.3 0.8 %shard_map.112 = (bf16[256,256]{1,0:T(8,128)(2,1)}, bf16[256,128]{1,0:T(8,128)(2,1)}, f32[128,256]{1,0:T(8,128)}, f32[1,256]{1,0:T(1,128)}) custom-call(bf16[256,256]{1,0:T(8,128)(2,1)S(1)} %get-tuple-element.12.refs_0_, bf16[256,128]{1,0:T(8,128)(2,1)S(1)} %get-tuple-element.13.refs_1_, f32[128,256]{1,0:T(8,128)S(1)} %get-tuple-element.14.refs_2_, ...), custom_call_target="tpu_custom_call" | custom-call | tf_op jit(solution)/shard_map/pallas_call | solution.py:584

commit v5 on v4

--- a/solution.py
+++ b/solution.py
@@ -160,8 +160,6 @@
             )
         )
     ]
-    for load in loads:
-        load.start()
 
     barrier = pltpu.get_barrier_semaphore()
     greet = [sibling, across] + [rid(0, d) for d in (1, 2, -1, -2)]
@@ -175,6 +173,8 @@
             barrier, inc=1, device_id={"row": row, "col": cid(*shift)},
             device_id_type=pl.DeviceIdType.MESH,
         )
+    for load in loads:
+        load.start()
     pl.semaphore_wait(barrier, len(greet) + len(shifts))
 
     def ag(a, dz, t, to, src=None):
@@ -381,8 +381,8 @@
             wcopy(wx_send, wx_recv.at[src], nz + n_col + j, rid(a, 0, other)).wait_recv()
         value = added(wx_recv, 4) * scale
         gb_ref[...] = value[chunk : chunk + 1, :]
-        wg_send[...] = value[:chunk, :]
-        wg_recv[z] = value[:chunk, :]
+        wg_send[...] = value[:chunk, :].astype(BF16)
+        wg_recv[z] = value[:chunk, :].astype(BF16)
         for d in far:
             go(wcopy(wg_send, wg_recv.at[z], nz + n_col + 4 + d, rid(0, d)))
 
@@ -391,7 +391,7 @@
             src = (z - d + nz) % nz
             wcopy(wg_send, wg_recv.at[src], nz + n_col + 4 + d, rid(0, -d)).wait_recv()
         for c in range(nz):
-            gw_ref[c * chunk : (c + 1) * chunk, :] = wg_recv[c]
+            gw_ref[c * chunk : (c + 1) * chunk, :] = wg_recv[c].astype(F32)
 
     order = [(1, 3), (1, -3), (1, 4), (0, 3), (0, -3), (0, 4), (1, 2), (1, -2)]
     order += [(1, 1), (1, -1), (0, 1), (0, -1), (0, 2), (0, -2), (1, 0), (0, 0)]
@@ -546,8 +546,8 @@
             pltpu.VMEM((n_col, chunk + 8, h), F32),
             pltpu.VMEM((chunk + 8, h), F32),
             pltpu.VMEM((4, chunk + 8, h), F32),
-            pltpu.VMEM((chunk, h), F32),
-            pltpu.VMEM((nz, chunk, h), F32),
+            pltpu.VMEM((chunk, h), BF16),
+            pltpu.VMEM((nz, chunk, h), BF16),
             dma((8,)),
             dma((4 * nz,)),
             dma((4 * nz,)),

time: 64.6 us -> 63.8 us (0.988)
  no operation moved by 1% of the time
where the time goes in v5:
time: 63.8 us; the launch traced here: 63.7 us
  Pallas kernels  62.4 us (98%)
  between operations  1.29 us (2%)
    pallas_call x1, Pallas kernels, local(): pl.pallas_call(functools.partial(kernel, n_row, n_col, scale), out_shape=...  61.7 us

profile of v5, /device:TPU:1, one launch (start us, length us, event | category | flops | bytes accessed | tf_op | source)
XLA Modules:
  0.0 63.7 jit_solution(8251161552995812839)
XLA Ops:
  1.3 61.7 %shard_map.111 = (bf16[256,256]{1,0:T(8,128)(2,1)S(1)}, bf16[256,128]{1,0:T(8,128)(2,1)S(1)}, f32[128,256]{1,0:T(8,128)S(1)}, f32[1,256]{1,0:T(1,128)S(1)}) custom-call(bf16[2,128,128]{2,1,0:T(8,128)(2,1)} %bitcast.7, bf16[128,256]{1,0:T(8,128)(2,1)} %w_hbm.1, f32[1,256]{1,0:T(1,128)} %bitcast.8, bf16[128,128,128]{2,1,0:T(8,128)(2,1)} %bitcast.6, ...), custom_call_target="tpu_custom_call" | custom-call | tf_op jit(solution)/shard_map/pallas_call | solution.py:515
  62.9 0.8 %shard_map.112 = (bf16[256,256]{1,0:T(8,128)(2,1)}, bf16[256,128]{1,0:T(8,128)(2,1)}, f32[128,256]{1,0:T(8,128)}, f32[1,256]{1,0:T(1,128)}) custom-call(bf16[256,256]{1,0:T(8,128)(2,1)S(1)} %get-tuple-element.12.refs_0_, bf16[256,128]{1,0:T(8,128)(2,1)S(1)} %get-tuple-element.13.refs_1_, f32[128,256]{1,0:T(8,128)S(1)} %get-tuple-element.14.refs_2_, ...), custom_call_target="tpu_custom_call" | custom-call | tf_op jit(solution)/shard_map/pallas_call | solution.py:584

commit v6 on v5

--- a/solution.py
+++ b/solution.py
@@ -10,7 +10,7 @@
 F32 = jnp.float32
 BF16 = jnp.bfloat16
 SIDE = 128
-UNROLL = 64
+UNROLL = 128
 
 
 def sort_plan(key, other, live, meta, base):
@@ -393,8 +393,8 @@
         for c in range(nz):
             gw_ref[c * chunk : (c + 1) * chunk, :] = wg_recv[c].astype(F32)
 
-    order = [(1, 3), (1, -3), (1, 4), (0, 3), (0, -3), (0, 4), (1, 2), (1, -2)]
-    order += [(1, 1), (1, -1), (0, 1), (0, -1), (0, 2), (0, -2), (1, 0), (0, 0)]
+    order = [(1, 3), (1, -3), (1, 4), (1, 2), (1, -2), (1, 1), (1, -1), (0, 3), (0, -3), (0, 4)]
+    order += [(1, 0), (0, 1), (0, -1), (0, 2), (0, -2), (0, 0)]
 
     def sib_copy(a, dz):
         k = a * nz + dz % nz
@@ -437,7 +437,7 @@
         ring(name, a, e, t, across).wait_recv()
         return ring_recv[slots[name, a, e], t].astype(F32)
 
-    for a in (1, 0):
+    for a in (1,):
         for e in signs:
             sib_copy(a, 3 * e).wait_recv()
             for t in (0, 1):
@@ -445,7 +445,20 @@
         sib_copy(a, 4).wait_recv()
         for t, e in enumerate((-1, 1)):
             ring_go("four", a, e, t, rid(0, 2 * e), comb(a, 4, t))
-    for a in (1, 0):
+    for a in (1,):
+        for e in signs:
+            sib_copy(a, e).wait_recv()
+            for t in (0, 1):
+                ring_go("one", a, e, t, rid(0, e), comb(a, e, t))
+    for a in (0,):
+        for e in signs:
+            sib_copy(a, 3 * e).wait_recv()
+            for t in (0, 1):
+                ring_go("three", a, e, t, rid(0, e), comb(a, 3 * e, t))
+        sib_copy(a, 4).wait_recv()
+        for t, e in enumerate((-1, 1)):
+            ring_go("four", a, e, t, rid(0, 2 * e), comb(a, 4, t))
+    for a in (0,):
         for e in signs:
             sib_copy(a, e).wait_recv()
             for t in (0, 1):

time: 63.8 us -> 63 us (0.987)
  Pallas kernels: 62.4 us -> 61.6 us
    pallas_call x1, Pallas kernels: 61.7 us -> 60.8 us  [local(): pl.pallas_call(functools.partial(kernel, n_row, n_col, scale), out_shape=...]
where the time goes in v6:
time: 63 us; the launch traced here: 62.9 us
  Pallas kernels  61.6 us (98%)
  between operations  1.29 us (2%)
    pallas_call x1, Pallas kernels, local(): pl.pallas_call(functools.partial(kernel, n_row, n_col, scale), out_shape=...  60.8 us

profile of v6, /device:TPU:1, one launch (start us, length us, event | category | flops | bytes accessed | tf_op | source)
XLA Modules:
  0.0 62.9 jit_solution(8926661046453398896)
XLA Ops:
  1.3 60.8 %shard_map.111 = (bf16[256,256]{1,0:T(8,128)(2,1)S(1)}, bf16[256,128]{1,0:T(8,128)(2,1)S(1)}, f32[128,256]{1,0:T(8,128)S(1)}, f32[1,256]{1,0:T(1,128)S(1)}) custom-call(bf16[2,128,128]{2,1,0:T(8,128)(2,1)} %bitcast.7, bf16[128,256]{1,0:T(8,128)(2,1)} %w_hbm.1, f32[1,256]{1,0:T(1,128)} %bitcast.8, bf16[128,128,128]{2,1,0:T(8,128)(2,1)} %bitcast.6, ...), custom_call_target="tpu_custom_call" | custom-call | tf_op jit(solution)/shard_map/pallas_call | solution.py:528
  62.1 0.8 %shard_map.112 = (bf16[256,256]{1,0:T(8,128)(2,1)}, bf16[256,128]{1,0:T(8,128)(2,1)}, f32[128,256]{1,0:T(8,128)}, f32[1,256]{1,0:T(1,128)}) custom-call(bf16[256,256]{1,0:T(8,128)(2,1)S(1)} %get-tuple-element.12.refs_0_, bf16[256,128]{1,0:T(8,128)(2,1)S(1)} %get-tuple-element.13.refs_1_, f32[128,256]{1,0:T(8,128)S(1)} %get-tuple-element.14.refs_2_, ...), custom_call_target="tpu_custom_call" | custom-call | tf_op jit(solution)/shard_map/pallas_call | solution.py:597

commit v7 on v6

--- a/solution.py
+++ b/solution.py
@@ -347,9 +347,9 @@
     products(5, False)
 
     def added(ref, n):
-        value = ref[0]
+        value = ref[0].astype(F32)
         for i in range(1, n):
-            value = value + ref[i]
+            value = value + ref[i].astype(F32)
         return value
 
     def over_z_done():
@@ -370,8 +370,8 @@
             src = cid(-dy, dx)
             wcopy(wc_send, wc_recv.at[src], nz + j, None, src).wait_recv()
         value = added(wc_recv, n_col)
-        wx_send[...] = value
-        wx_recv[quad] = value
+        wx_send[...] = jnp.concatenate([value, value[chunk:, :]], axis=0).astype(BF16)
+        wx_recv[quad] = wx_send[...]
         for j, (a, other) in enumerate(quads):
             go(wcopy(wx_send, wx_recv.at[quad], nz + n_col + j, rid(a, 0, other)))
 
@@ -557,8 +557,8 @@
             pltpu.VMEM((nz, chunk + 8, h), F32),
             pltpu.VMEM((chunk + 8, h), F32),
             pltpu.VMEM((n_col, chunk + 8, h), F32),
-            pltpu.VMEM((chunk + 8, h), F32),
-            pltpu.VMEM((4, chunk + 8, h), F32),
+            pltpu.VMEM((chunk + 16, h), BF16),
+            pltpu.VMEM((4, chunk + 16, h), BF16),
             pltpu.VMEM((chunk, h), BF16),
             pltpu.VMEM((nz, chunk, h), BF16),
             dma((8,)),

time: 63 us -> 63 us (level)
  no operation moved by 1% of the time
where the time goes in v7:
time: 63 us; the launch traced here: 62.9 us
  Pallas kernels  61.6 us (98%)
  between operations  1.29 us (2%)
    pallas_call x1, Pallas kernels, local(): pl.pallas_call(functools.partial(kernel, n_row, n_col, scale), out_shape=...  60.8 us

profile of v7, /device:TPU:1, one launch (start us, length us, event | category | flops | bytes accessed | tf_op | source)
XLA Modules:
  0.0 62.9 jit_solution(16211819525680200025)
XLA Ops:
  1.3 60.8 %shard_map.111 = (bf16[256,256]{1,0:T(8,128)(2,1)S(1)}, bf16[256,128]{1,0:T(8,128)(2,1)S(1)}, f32[128,256]{1,0:T(8,128)S(1)}, f32[1,256]{1,0:T(1,128)S(1)}) custom-call(bf16[2,128,128]{2,1,0:T(8,128)(2,1)} %bitcast.7, bf16[128,256]{1,0:T(8,128)(2,1)} %w_hbm.1, f32[1,256]{1,0:T(1,128)} %bitcast.8, bf16[128,128,128]{2,1,0:T(8,128)(2,1)} %bitcast.6, ...), custom_call_target="tpu_custom_call" | custom-call | tf_op jit(solution)/shard_map/pallas_call | solution.py:528
  62.1 0.8 %shard_map.112 = (bf16[256,256]{1,0:T(8,128)(2,1)}, bf16[256,128]{1,0:T(8,128)(2,1)}, f32[128,256]{1,0:T(8,128)}, f32[1,256]{1,0:T(1,128)}) custom-call(bf16[256,256]{1,0:T(8,128)(2,1)S(1)} %get-tuple-element.12.refs_0_, bf16[256,128]{1,0:T(8,128)(2,1)S(1)} %get-tuple-element.13.refs_1_, f32[128,256]{1,0:T(8,128)S(1)} %get-tuple-element.14.refs_2_, ...), custom_call_target="tpu_custom_call" | custom-call | tf_op jit(solution)/shard_map/pallas_call | solution.py:597
